TPU v7x, 32 devices: a whole 2x2x4 slice. The times are simulated.
32 devices in a mesh: section: 4 (over y, x), lon: 8 (over z, core).
Axes of the slice: x: 2, y: 2, z: 4, core: 2. Of those that a mesh axis runs over, the one named last changes fastest.
Arguments:
- section_inputs: bfloat16 [4, 2, 32, 64, 256], P('section', None, None, 'lon'), may hold values from -6 to 6
- weights: bfloat16 [4, 2, 3, 3, 256, 256], P('section'), may hold values from -0.125 to 0.125
- out_cot: bfloat16 [2, 32, 64, 256], P(None, None, 'lon'), may hold values from -6 to 6
Outputs:
- act_grads: bfloat16 [4, 2, 32, 64, 256], P('section', None, None, 'lon')
- weight_grads: float32 [4, 2, 3, 3, 256, 256], P('section')
All inputs are finite; a program needn't handle non-finite values.
Results may differ from a plain program's by a relative error of at most 0.02.
Values may be sent and summed in bfloat16 or wider, within the bound.
A program may use at most 64 MiB of HBM per device.

v0:
```python
import math

import jax
import jax.numpy as jnp
from jax import lax
from jax.sharding import PartitionSpec as P


def extended(cells, sides, width):
    for axis, dim in sides:
        count = lax.axis_size(axis)
        head = lax.slice_in_dim(cells, 0, width, axis=dim)
        tail = lax.slice_in_dim(cells, cells.shape[dim] - width, cells.shape[dim], axis=dim)
        cells = jnp.concatenate(
            [
                lax.ppermute(tail, axis, [(i, (i + 1) % count) for i in range(count)]),
                cells,
                lax.ppermute(head, axis, [((i + 1) % count, i) for i in range(count)]),
            ],
            axis=dim,
        )
    return cells


def from_behind(array, axis, by):
    size = lax.axis_size(axis)
    pairs = [(i, i + by) for i in range(size) if 0 <= i + by < size]
    return lax.ppermute(array, axis, pairs)


def lat_pad(field):
    return jnp.pad(field, ((1, 1), (0, 0), (0, 0)))


def convolve(padded, kernel):
    row_count = padded.shape[0] - 2
    col_count = padded.shape[1] - 2
    channels = padded.shape[2]
    running = jnp.zeros((row_count * col_count, kernel.shape[3]), jnp.float32)
    for lat_off in range(3):
        for lon_off in range(3):
            window = padded[lat_off : lat_off + row_count, lon_off : lon_off + col_count].reshape(
                -1, channels
            )
            running = running + jnp.dot(
                window, kernel[lat_off, lon_off], preferred_element_type=jnp.float32
            )
    return running.reshape(row_count, col_count, -1)


def convolve_back(padded, kernel):
    row_count = padded.shape[0] - 2
    col_count = padded.shape[1] - 2
    channels = padded.shape[2]
    running = jnp.zeros((row_count * col_count, kernel.shape[2]), jnp.float32)
    for lat_off in range(3):
        for lon_off in range(3):
            window = padded[
                2 - lat_off : 2 - lat_off + row_count, 2 - lon_off : 2 - lon_off + col_count
            ].reshape(-1, channels)
            running = running + lax.dot_general(
                window,
                kernel[lat_off, lon_off],
                (((1,), (1,)), ((), ())),
                preferred_element_type=jnp.float32,
            )
    return running.reshape(row_count, col_count, -1)


def correlate(padded, grad):
    row_count = grad.shape[0]
    col_count = grad.shape[1]
    channels = padded.shape[2]
    flat_grad = grad.reshape(-1, grad.shape[2])
    outer = []
    for lat_off in range(3):
        inner = []
        for lon_off in range(3):
            window = padded[lat_off : lat_off + row_count, lon_off : lon_off + col_count].reshape(
                -1, channels
            )
            inner.append(
                lax.dot_general(
                    window, flat_grad, (((0,), (0,)), ((), ())), preferred_element_type=jnp.float32
                )
            )
        outer.append(jnp.stack(inner))
    return jnp.stack(outer)


def silu_slope(preact):
    sig = jax.nn.sigmoid(preact)
    return sig * (1.0 + preact * (1.0 - sig))


def local(section_inputs, weights, out_cot):
    inputs_here = section_inputs[0]
    kernel_one = weights[0, 0]
    kernel_two = weights[0, 1]
    micro_count, row_count, col_count, channels = inputs_here.shape
    section_count = lax.axis_size("section")
    section_idx = lax.axis_index("section")
    factor = 1.0 / math.sqrt(micro_count * row_count * col_count * lax.axis_size("lon"))
    turn_count = section_count + micro_count - 1
    margin = 1

    def one_turn(turn, state):
        received, grad_one, grad_two, act_out = state
        batch_idx = turn - (section_count - 1 - section_idx)
        active = (batch_idx >= 0) & (batch_idx < micro_count)
        picked = jnp.clip(batch_idx, 0, micro_count - 1)
        last_cot = lax.dynamic_index_in_dim(out_cot, picked, 0, keepdims=False)
        cotangent = jnp.where(section_idx == section_count - 1, last_cot, received)
        input_now = lax.dynamic_index_in_dim(inputs_here, picked, 0, keepdims=False)
        input_ext = extended(input_now, (("lon", 1),), margin)
        padded_in = lat_pad(input_ext)
        preact = convolve(padded_in, kernel_one)
        hidden = jax.nn.silu(preact).astype(jnp.bfloat16)
        hidden_ext = extended(hidden, (("lon", 1),), 1)
        padded_hidden = lat_pad(hidden_ext)
        padded_cot = lat_pad(extended(cotangent, (("lon", 1),), 1))
        hidden_grad = convolve_back(padded_cot, kernel_two)
        preact_grad = (hidden_grad * silu_slope(preact)).astype(jnp.bfloat16)
        padded_grad = lat_pad(extended(preact_grad, (("lon", 1),), 1))
        input_grad = (
            cotangent.astype(jnp.float32) + convolve_back(padded_grad, kernel_one)
        ).astype(jnp.bfloat16)
        weight_mask = active.astype(jnp.float32)
        grad_two = grad_two + weight_mask * correlate(padded_hidden, cotangent)
        grad_one = grad_one + weight_mask * correlate(padded_in, preact_grad)
        updated = lax.dynamic_update_index_in_dim(act_out, input_grad, picked, 0)
        act_out = jnp.where(active, updated, act_out)
        received = from_behind(input_grad, "section", -1)
        return (received, grad_one, grad_two, act_out)

    start_state = (
        jnp.zeros((row_count, col_count, channels), jnp.bfloat16),
        jnp.zeros((3, 3, channels, channels), jnp.float32),
        jnp.zeros((3, 3, channels, channels), jnp.float32),
        jnp.zeros((micro_count, row_count, col_count, channels), jnp.bfloat16),
    )
    received, grad_one, grad_two, act_out = lax.fori_loop(0, turn_count, one_turn, start_state)
    summed_one, summed_two = lax.psum((grad_one, grad_two), "lon")
    weight_grads = (jnp.stack([summed_one, summed_two]) * factor)[None]
    return (act_out[None], weight_grads)


def solution(mesh):
    placed = (
        P("section", None, None, "lon", None),
        P("section", None, None, None, None, None),
        P(None, None, "lon", None),
    )
    return jax.shard_map(
        local,
        mesh=mesh,
        in_specs=placed,
        out_specs=(
            P("section", None, None, "lon", None),
            P("section", None, None, None, None, None),
        ),
        check_vma=False,
    )
```

profile of v0, /device:TPU:0, one launch (start us, length us, event | category | flops | bytes accessed | tf_op | source)
XLA Modules:
  0.0 336.6 jit_solution(98441229511830247)
XLA Ops:
  7.2 1.8 slice_bitcast_fusion.12
  9.1 206.4 %while.22 = (s32[]{:T(128)}, bf16[32,8,256]{2,1,0:T(8,128)(2,1)S(1)}, f32[3,3,256,256]{3,2,1,0:T(8,128)}, f32[3,3,256,256]{3,2,1,0:T(8,128)}, bf16[2,32,8,256]{3...) while((s32[]{:T(128)}, ...), condition=%wide.region_1.2_spmd.clone, body=%wide.region_0.1_spmd.clone.sunk | while | flops 1527562240 | bytes 100377280 | solution.py:142
  10.1 4.5 %collective-permute-start = (bf16[32,1,256]{2,0,1:T(8,128)(2,1)S(1)}, bf16[32,1,256]{2,0,1:T(8,128)(2,1)S(1)}, u32[]{:S(2)}, u32[]{:S(2)}) collective-permute-start(bf16[32,1,256]{2,0,1:T(8,128)(2,1)S(1)} %get-tuple-element.464), channel_id=1, source_target_pairs={{1,0},{2,1},{3,2},{4,3},{5,4},{6,5},{7,6},{0,7},{9,8},{10,9},{11,1... | collective-permute-start | bytes 49160 | tf_op jit(solution)/shard_map/while/body/eval_jaxpr/ppermute | solution.py:18
  15.6 3.6 %collective-permute-start.2 = (bf16[32,1,256]{2,1,0:T(2,128)(2,1)S(1)}, bf16[32,1,256]{2,1,0:T(2,128)(2,1)S(1)}, u32[]{:S(2)}, u32[]{:S(2)}) collective-permute-start(bf16[32,1,256]{2,1,0:T(2,128)(2,1)S(1)} %get-tuple-element.474), channel_id=1, source_target_pairs={{1,0},{2,1},{3,2},{4,3},{5,4},{6,5},{7,6},{0,7},{9,8},{10,9},{11,1... | collective-permute-start | bytes 49160 | tf_op jit(solution)/shard_map/while/body/eval_jaxpr/ppermute | solution.py:18
  19.4 1.4 collective-permute-done.2
  20.8 3.5 %collective-permute-done.3 = bf16[32,1,256]{2,1,0:T(2,128)(2,1)S(1)} collective-permute-done((bf16[32,1,256]{2,1,0:T(2,128)(2,1)S(1)}, bf16[32,1,256]{2,1,0:T(2,128)(2,1)S(1)}, u32[]{:S(2)}, u32[]{:S(2)}) %collective-permute-start.3) | collective-permute-done | bytes 16416 | tf_op jit(solution)/shard_map/while/body/eval_jaxpr/ppermute | solution.py:16
  30.4 3.6 %collective-permute-start.7 = (bf16[32,1,256]{2,0,1:T(8,128)(2,1)S(1)}, bf16[32,1,256]{2,0,1:T(8,128)(2,1)S(1)}, u32[]{:S(2)}, u32[]{:S(2)}) collective-permute-start(bf16[32,1,256]{2,0,1:T(8,128)(2,1)S(1)} %get-tuple-element.493), channel_id=1, source_target_pairs={{1,0},{2,1},{3,2},{4,3},{5,4},{6,5},{7,6},{0,7},{9,8},{10,9},{11,1... | collective-permute-start | bytes 49160 | tf_op jit(solution)/shard_map/while/body/eval_jaxpr/ppermute | solution.py:18
  34.6 1.5 copy-done
  37.3 3.6 %collective-permute-start.4 = (bf16[32,1,256]{2,0,1:T(8,128)(2,1)S(1)}, bf16[32,1,256]{2,0,1:T(8,128)(2,1)S(1)}, u32[]{:S(2)}, u32[]{:S(2)}) collective-permute-start(bf16[32,1,256]{2,0,1:T(8,128)(2,1)S(1)} %get-tuple-element.478), channel_id=1, source_target_pairs={{1,0},{2,1},{3,2},{4,3},{5,4},{6,5},{7,6},{0,7},{9,8},{10,9},{11,1... | collective-permute-start | bytes 49160 | tf_op jit(solution)/shard_map/while/body/eval_jaxpr/ppermute | solution.py:18
  46.6 1.5 copy-done.2
  49.0 2.5 collective-permute-done.6
  52.5 2.4 collective-permute-start
  55.8 3.6 %collective-permute-start.2 = (bf16[32,1,256]{2,1,0:T(2,128)(2,1)S(1)}, bf16[32,1,256]{2,1,0:T(2,128)(2,1)S(1)}, u32[]{:S(2)}, u32[]{:S(2)}) collective-permute-start(bf16[32,1,256]{2,1,0:T(2,128)(2,1)S(1)} %get-tuple-element.474), channel_id=1, source_target_pairs={{1,0},{2,1},{3,2},{4,3},{5,4},{6,5},{7,6},{0,7},{9,8},{10,9},{11,1... | collective-permute-start | bytes 49160 | tf_op jit(solution)/shard_map/while/body/eval_jaxpr/ppermute | solution.py:18
  61.0 3.5 %collective-permute-done.3 = bf16[32,1,256]{2,1,0:T(2,128)(2,1)S(1)} collective-permute-done((bf16[32,1,256]{2,1,0:T(2,128)(2,1)S(1)}, bf16[32,1,256]{2,1,0:T(2,128)(2,1)S(1)}, u32[]{:S(2)}, u32[]{:S(2)}) %collective-permute-start.3) | collective-permute-done | bytes 16416 | tf_op jit(solution)/shard_map/while/body/eval_jaxpr/ppermute | solution.py:16
  70.7 3.6 %collective-permute-start.7 = (bf16[32,1,256]{2,0,1:T(8,128)(2,1)S(1)}, bf16[32,1,256]{2,0,1:T(8,128)(2,1)S(1)}, u32[]{:S(2)}, u32[]{:S(2)}) collective-permute-start(bf16[32,1,256]{2,0,1:T(8,128)(2,1)S(1)} %get-tuple-element.493), channel_id=1, source_target_pairs={{1,0},{2,1},{3,2},{4,3},{5,4},{6,5},{7,6},{0,7},{9,8},{10,9},{11,1... | collective-permute-start | bytes 49160 | tf_op jit(solution)/shard_map/while/body/eval_jaxpr/ppermute | solution.py:18
  74.9 1.5 copy-done
  77.5 3.6 %collective-permute-start.4 = (bf16[32,1,256]{2,0,1:T(8,128)(2,1)S(1)}, bf16[32,1,256]{2,0,1:T(8,128)(2,1)S(1)}, u32[]{:S(2)}, u32[]{:S(2)}) collective-permute-start(bf16[32,1,256]{2,0,1:T(8,128)(2,1)S(1)} %get-tuple-element.478), channel_id=1, source_target_pairs={{1,0},{2,1},{3,2},{4,3},{5,4},{6,5},{7,6},{0,7},{9,8},{10,9},{11,1... | collective-permute-start | bytes 49160 | tf_op jit(solution)/shard_map/while/body/eval_jaxpr/ppermute | solution.py:18
  86.8 1.5 copy-done.2
  89.2 2.9 collective-permute-done.6
  93.1 2.7 collective-permute-start
  96.7 3.6 %collective-permute-start.2 = (bf16[32,1,256]{2,1,0:T(2,128)(2,1)S(1)}, bf16[32,1,256]{2,1,0:T(2,128)(2,1)S(1)}, u32[]{:S(2)}, u32[]{:S(2)}) collective-permute-start(bf16[32,1,256]{2,1,0:T(2,128)(2,1)S(1)} %get-tuple-element.474), channel_id=1, source_target_pairs={{1,0},{2,1},{3,2},{4,3},{5,4},{6,5},{7,6},{0,7},{9,8},{10,9},{11,1... | collective-permute-start | bytes 49160 | tf_op jit(solution)/shard_map/while/body/eval_jaxpr/ppermute | solution.py:18
  100.5 1.4 collective-permute-done.2
  101.9 3.5 %collective-permute-done.3 = bf16[32,1,256]{2,1,0:T(2,128)(2,1)S(1)} collective-permute-done((bf16[32,1,256]{2,1,0:T(2,128)(2,1)S(1)}, bf16[32,1,256]{2,1,0:T(2,128)(2,1)S(1)}, u32[]{:S(2)}, u32[]{:S(2)}) %collective-permute-start.3) | collective-permute-done | bytes 16416 | tf_op jit(solution)/shard_map/while/body/eval_jaxpr/ppermute | solution.py:16
  111.5 3.6 %collective-permute-start.7 = (bf16[32,1,256]{2,0,1:T(8,128)(2,1)S(1)}, bf16[32,1,256]{2,0,1:T(8,128)(2,1)S(1)}, u32[]{:S(2)}, u32[]{:S(2)}) collective-permute-start(bf16[32,1,256]{2,0,1:T(8,128)(2,1)S(1)} %get-tuple-element.493), channel_id=1, source_target_pairs={{1,0},{2,1},{3,2},{4,3},{5,4},{6,5},{7,6},{0,7},{9,8},{10,9},{11,1... | collective-permute-start | bytes 49160 | tf_op jit(solution)/shard_map/while/body/eval_jaxpr/ppermute | solution.py:18
  115.7 1.5 copy-done
  118.3 3.6 %collective-permute-start.4 = (bf16[32,1,256]{2,0,1:T(8,128)(2,1)S(1)}, bf16[32,1,256]{2,0,1:T(8,128)(2,1)S(1)}, u32[]{:S(2)}, u32[]{:S(2)}) collective-permute-start(bf16[32,1,256]{2,0,1:T(8,128)(2,1)S(1)} %get-tuple-element.478), channel_id=1, source_target_pairs={{1,0},{2,1},{3,2},{4,3},{5,4},{6,5},{7,6},{0,7},{9,8},{10,9},{11,1... | collective-permute-start | bytes 49160 | tf_op jit(solution)/shard_map/while/body/eval_jaxpr/ppermute | solution.py:18
  127.7 1.5 copy-done.2
  130.1 3.2 collective-permute-done.6
  134.2 2.7 collective-permute-start
  137.8 3.6 %collective-permute-start.2 = (bf16[32,1,256]{2,1,0:T(2,128)(2,1)S(1)}, bf16[32,1,256]{2,1,0:T(2,128)(2,1)S(1)}, u32[]{:S(2)}, u32[]{:S(2)}) collective-permute-start(bf16[32,1,256]{2,1,0:T(2,128)(2,1)S(1)} %get-tuple-element.474), channel_id=1, source_target_pairs={{1,0},{2,1},{3,2},{4,3},{5,4},{6,5},{7,6},{0,7},{9,8},{10,9},{11,1... | collective-permute-start | bytes 49160 | tf_op jit(solution)/shard_map/while/body/eval_jaxpr/ppermute | solution.py:18
  141.7 1.4 collective-permute-done.2
  143.0 3.5 %collective-permute-done.3 = bf16[32,1,256]{2,1,0:T(2,128)(2,1)S(1)} collective-permute-done((bf16[32,1,256]{2,1,0:T(2,128)(2,1)S(1)}, bf16[32,1,256]{2,1,0:T(2,128)(2,1)S(1)}, u32[]{:S(2)}, u32[]{:S(2)}) %collective-permute-start.3) | collective-permute-done | bytes 16416 | tf_op jit(solution)/shard_map/while/body/eval_jaxpr/ppermute | solution.py:16
  152.6 3.6 %collective-permute-start.7 = (bf16[32,1,256]{2,0,1:T(8,128)(2,1)S(1)}, bf16[32,1,256]{2,0,1:T(8,128)(2,1)S(1)}, u32[]{:S(2)}, u32[]{:S(2)}) collective-permute-start(bf16[32,1,256]{2,0,1:T(8,128)(2,1)S(1)} %get-tuple-element.493), channel_id=1, source_target_pairs={{1,0},{2,1},{3,2},{4,3},{5,4},{6,5},{7,6},{0,7},{9,8},{10,9},{11,1... | collective-permute-start | bytes 49160 | tf_op jit(solution)/shard_map/while/body/eval_jaxpr/ppermute | solution.py:18
  156.9 1.5 copy-done
  159.5 3.6 %collective-permute-start.4 = (bf16[32,1,256]{2,0,1:T(8,128)(2,1)S(1)}, bf16[32,1,256]{2,0,1:T(8,128)(2,1)S(1)}, u32[]{:S(2)}, u32[]{:S(2)}) collective-permute-start(bf16[32,1,256]{2,0,1:T(8,128)(2,1)S(1)} %get-tuple-element.478), channel_id=1, source_target_pairs={{1,0},{2,1},{3,2},{4,3},{5,4},{6,5},{7,6},{0,7},{9,8},{10,9},{11,1... | collective-permute-start | bytes 49160 | tf_op jit(solution)/shard_map/while/body/eval_jaxpr/ppermute | solution.py:18
  168.8 1.5 copy-done.2
  171.2 3.2 collective-permute-done.6
  175.3 2.7 collective-permute-start
  178.9 3.6 %collective-permute-start.2 = (bf16[32,1,256]{2,1,0:T(2,128)(2,1)S(1)}, bf16[32,1,256]{2,1,0:T(2,128)(2,1)S(1)}, u32[]{:S(2)}, u32[]{:S(2)}) collective-permute-start(bf16[32,1,256]{2,1,0:T(2,128)(2,1)S(1)} %get-tuple-element.474), channel_id=1, source_target_pairs={{1,0},{2,1},{3,2},{4,3},{5,4},{6,5},{7,6},{0,7},{9,8},{10,9},{11,1... | collective-permute-start | bytes 49160 | tf_op jit(solution)/shard_map/while/body/eval_jaxpr/ppermute | solution.py:18
  182.8 1.4 collective-permute-done.2
  184.1 3.5 %collective-permute-done.3 = bf16[32,1,256]{2,1,0:T(2,128)(2,1)S(1)} collective-permute-done((bf16[32,1,256]{2,1,0:T(2,128)(2,1)S(1)}, bf16[32,1,256]{2,1,0:T(2,128)(2,1)S(1)}, u32[]{:S(2)}, u32[]{:S(2)}) %collective-permute-start.3) | collective-permute-done | bytes 16416 | tf_op jit(solution)/shard_map/while/body/eval_jaxpr/ppermute | solution.py:16
  193.8 3.6 %collective-permute-start.7 = (bf16[32,1,256]{2,0,1:T(8,128)(2,1)S(1)}, bf16[32,1,256]{2,0,1:T(8,128)(2,1)S(1)}, u32[]{:S(2)}, u32[]{:S(2)}) collective-permute-start(bf16[32,1,256]{2,0,1:T(8,128)(2,1)S(1)} %get-tuple-element.493), channel_id=1, source_target_pairs={{1,0},{2,1},{3,2},{4,3},{5,4},{6,5},{7,6},{0,7},{9,8},{10,9},{11,1... | collective-permute-start | bytes 49160 | tf_op jit(solution)/shard_map/while/body/eval_jaxpr/ppermute | solution.py:18
  198.0 1.5 copy-done
  200.6 3.6 %collective-permute-start.4 = (bf16[32,1,256]{2,0,1:T(8,128)(2,1)S(1)}, bf16[32,1,256]{2,0,1:T(8,128)(2,1)S(1)}, u32[]{:S(2)}, u32[]{:S(2)}) collective-permute-start(bf16[32,1,256]{2,0,1:T(8,128)(2,1)S(1)} %get-tuple-element.478), channel_id=1, source_target_pairs={{1,0},{2,1},{3,2},{4,3},{5,4},{6,5},{7,6},{0,7},{9,8},{10,9},{11,1... | collective-permute-start | bytes 49160 | tf_op jit(solution)/shard_map/while/body/eval_jaxpr/ppermute | solution.py:18
  209.9 1.5 copy-done.2
  212.3 3.2 collective-permute-done.6
  216.2 108.6 %all-reduce.7.cloned.1.call-done = (f32[1,1,3,3,256,256]{5,4,3,2,1,0:T(8,128)}, f32[1,1,3,3,256,256]{5,4,3,2,1,0:T(8,128)}) async-done(((f32[1,1,3,3,256,256]{5,4,3,2,1,0:T(8,128)}, f32[1,1,3,3,256,256]{5,4,3,2,1,0:T(8,128)}), (f32[1,1,3,3,256,256]{5,4,3,2,1,0:T(8,128)}, f32[1,1,3,3,256,256]{5,4,3,2,1,0:T(8,128)})) %all-reduce.7.cloned.1.call-update) | async-done | bytes 4718608 | tf_op jit(solution)/shard_map/psum | solution.py:143
  324.8 5.0 %maximum_multiply_fusion.2 = f32[1,2,3,3,256,256]{5,4,3,2,1,0:T(8,128)} fusion(f32[1,1,3,3,256,256]{5,4,3,2,1,0:T(8,128)} %get-tuple-element.325, f32[1,1,3,3,256,256]{5,4,3,2,1,0:T(8,128)} %get-tuple-element.326), kind=kLoop, calls=%fused_computation.234 | loop fusion | flops 2359296 | bytes 9437184 | tf_op jit(solution)/shard_map/mul | solution.py:144
  (429 shorter events, 82.1 us)
Async XLA Ops:
  7.2 317.6 %all-reduce.7.cloned.1.call-start = ((), (), s32[]{:S(2)}) async-start(), calls=%async_computation | async-start | bytes 9437184 | tf_op jit(solution)/shard_map/psum | solution.py:143
  10.1 14.9 %collective-permute-start = (bf16[32,1,256]{2,0,1:T(8,128)(2,1)S(1)}, bf16[32,1,256]{2,0,1:T(8,128)(2,1)S(1)}, u32[]{:S(2)}, u32[]{:S(2)}) collective-permute-start(bf16[32,1,256]{2,0,1:T(8,128)(2,1)S(1)} %get-tuple-element.464), channel_id=1, source_target_pairs={{1,0},{2,1},{3,2},{4,3},{5,4},{6,5},{7,6},{0,7},{9,8},{10,9},{11,1... | collective-permute-start | bytes 49160 | tf_op jit(solution)/shard_map/while/body/eval_jaxpr/ppermute | solution.py:18
  14.6 10.3 %collective-permute-start.1 = (bf16[32,1,256]{2,0,1:T(8,128)(2,1)S(1)}, bf16[32,1,256]{2,0,1:T(8,128)(2,1)S(1)}, u32[]{:S(2)}, u32[]{:S(2)}) collective-permute-start(bf16[32,1,256]{2,0,1:T(8,128)(2,1)S(1)} %get-tuple-element.465), channel_id=1, source_target_pairs={{0,1},{1,2},{2,3},{3,4},{4,5},{5,6},{6,7},{7,0},{8,9},{9,10},{10,1... | collective-permute-start | bytes 49160 | tf_op jit(solution)/shard_map/while/body/eval_jaxpr/ppermute | solution.py:16
  15.6 5.2 %collective-permute-start.2 = (bf16[32,1,256]{2,1,0:T(2,128)(2,1)S(1)}, bf16[32,1,256]{2,1,0:T(2,128)(2,1)S(1)}, u32[]{:S(2)}, u32[]{:S(2)}) collective-permute-start(bf16[32,1,256]{2,1,0:T(2,128)(2,1)S(1)} %get-tuple-element.474), channel_id=1, source_target_pairs={{1,0},{2,1},{3,2},{4,3},{5,4},{6,5},{7,6},{0,7},{9,8},{10,9},{11,1... | collective-permute-start | bytes 49160 | tf_op jit(solution)/shard_map/while/body/eval_jaxpr/ppermute | solution.py:18
  19.2 5.1 %collective-permute-start.3 = (bf16[32,1,256]{2,1,0:T(2,128)(2,1)S(1)}, bf16[32,1,256]{2,1,0:T(2,128)(2,1)S(1)}, u32[]{:S(2)}, u32[]{:S(2)}) collective-permute-start(bf16[32,1,256]{2,1,0:T(2,128)(2,1)S(1)} %get-tuple-element.475), channel_id=1, source_target_pairs={{0,1},{1,2},{2,3},{3,4},{4,5},{5,6},{6,7},{7,0},{8,9},{9,10},{10,1... | collective-permute-start | bytes 49160 | tf_op jit(solution)/shard_map/while/body/eval_jaxpr/ppermute | solution.py:16
  30.1 12.2 %collective-permute-start.5 = (bf16[32,1,256]{2,0,1:T(8,128)(2,1)S(1)}, bf16[32,1,256]{2,0,1:T(8,128)(2,1)S(1)}, u32[]{:S(2)}, u32[]{:S(2)}) collective-permute-start(bf16[32,1,256]{2,0,1:T(8,128)(2,1)S(1)} %get-tuple-element.479), channel_id=1, source_target_pairs={{0,1},{1,2},{2,3},{3,4},{4,5},{5,6},{6,7},{7,0},{8,9},{9,10},{10,1... | collective-permute-start | bytes 49160 | tf_op jit(solution)/shard_map/while/body/eval_jaxpr/ppermute | solution.py:16
  30.4 10.4 %collective-permute-start.7 = (bf16[32,1,256]{2,0,1:T(8,128)(2,1)S(1)}, bf16[32,1,256]{2,0,1:T(8,128)(2,1)S(1)}, u32[]{:S(2)}, u32[]{:S(2)}) collective-permute-start(bf16[32,1,256]{2,0,1:T(8,128)(2,1)S(1)} %get-tuple-element.493), channel_id=1, source_target_pairs={{1,0},{2,1},{3,2},{4,3},{5,4},{6,5},{7,6},{0,7},{9,8},{10,9},{11,1... | collective-permute-start | bytes 49160 | tf_op jit(solution)/shard_map/while/body/eval_jaxpr/ppermute | solution.py:18
  34.0 6.9 %collective-permute-start.8 = (bf16[32,1,256]{2,0,1:T(8,128)(2,1)S(1)}, bf16[32,1,256]{2,0,1:T(8,128)(2,1)S(1)}, u32[]{:S(2)}, u32[]{:S(2)}) collective-permute-start(bf16[32,1,256]{2,0,1:T(8,128)(2,1)S(1)} %get-tuple-element.494), channel_id=1, source_target_pairs={{0,1},{1,2},{2,3},{3,4},{4,5},{5,6},{6,7},{7,0},{8,9},{9,10},{10,1... | collective-permute-start | bytes 49160 | tf_op jit(solution)/shard_map/while/body/eval_jaxpr/ppermute | solution.py:16
  37.0 4.4 %copy-start.1 = (f32[3,3,256,256]{3,2,1,0:T(8,128)}, f32[3,3,256,256]{3,2,1,0:T(8,128)S(1)}, u32[]{:S(2)}) copy-start(f32[3,3,256,256]{3,2,1,0:T(8,128)S(1)} %fusion.369) | copy-start | bytes 7077892 | tf_op jit(solution)/shard_map/while
  37.3 5.1 %collective-permute-start.4 = (bf16[32,1,256]{2,0,1:T(8,128)(2,1)S(1)}, bf16[32,1,256]{2,0,1:T(8,128)(2,1)S(1)}, u32[]{:S(2)}, u32[]{:S(2)}) collective-permute-start(bf16[32,1,256]{2,0,1:T(8,128)(2,1)S(1)} %get-tuple-element.478), channel_id=1, source_target_pairs={{1,0},{2,1},{3,2},{4,3},{5,4},{6,5},{7,6},{0,7},{9,8},{10,9},{11,1... | collective-permute-start | bytes 49160 | tf_op jit(solution)/shard_map/while/body/eval_jaxpr/ppermute | solution.py:18
  44.6 6.9 %collective-permute-start.6 = (bf16[32,8,256]{2,1,0:T(8,128)(2,1)S(1)}, bf16[32,8,256]{2,1,0:T(8,128)(2,1)S(1)}, u32[]{:S(2)}, u32[]{:S(2)}) collective-permute-start(bf16[32,8,256]{2,1,0:T(8,128)(2,1)S(1)} %get-tuple-element.489), channel_id=1, source_target_pairs={{8,0},{16,8},{24,16},{9,1},{17,9},{25,17},{10,2},{18,10},{26,18},{... | collective-permute-start | bytes 393224 | tf_op jit(solution)/shard_map/while/body/eval_jaxpr/ppermute | solution.py:28
  52.5 12.7 %collective-permute-start = (bf16[32,1,256]{2,0,1:T(8,128)(2,1)S(1)}, bf16[32,1,256]{2,0,1:T(8,128)(2,1)S(1)}, u32[]{:S(2)}, u32[]{:S(2)}) collective-permute-start(bf16[32,1,256]{2,0,1:T(8,128)(2,1)S(1)} %get-tuple-element.464), channel_id=1, source_target_pairs={{1,0},{2,1},{3,2},{4,3},{5,4},{6,5},{7,6},{0,7},{9,8},{10,9},{11,1... | collective-permute-start | bytes 49160 | tf_op jit(solution)/shard_map/while/body/eval_jaxpr/ppermute | solution.py:18
  54.9 10.3 %collective-permute-start.1 = (bf16[32,1,256]{2,0,1:T(8,128)(2,1)S(1)}, bf16[32,1,256]{2,0,1:T(8,128)(2,1)S(1)}, u32[]{:S(2)}, u32[]{:S(2)}) collective-permute-start(bf16[32,1,256]{2,0,1:T(8,128)(2,1)S(1)} %get-tuple-element.465), channel_id=1, source_target_pairs={{0,1},{1,2},{2,3},{3,4},{4,5},{5,6},{6,7},{7,0},{8,9},{9,10},{10,1... | collective-permute-start | bytes 49160 | tf_op jit(solution)/shard_map/while/body/eval_jaxpr/ppermute | solution.py:16
  55.8 5.2 %collective-permute-start.2 = (bf16[32,1,256]{2,1,0:T(2,128)(2,1)S(1)}, bf16[32,1,256]{2,1,0:T(2,128)(2,1)S(1)}, u32[]{:S(2)}, u32[]{:S(2)}) collective-permute-start(bf16[32,1,256]{2,1,0:T(2,128)(2,1)S(1)} %get-tuple-element.474), channel_id=1, source_target_pairs={{1,0},{2,1},{3,2},{4,3},{5,4},{6,5},{7,6},{0,7},{9,8},{10,9},{11,1... | collective-permute-start | bytes 49160 | tf_op jit(solution)/shard_map/while/body/eval_jaxpr/ppermute | solution.py:18
  59.4 5.1 %collective-permute-start.3 = (bf16[32,1,256]{2,1,0:T(2,128)(2,1)S(1)}, bf16[32,1,256]{2,1,0:T(2,128)(2,1)S(1)}, u32[]{:S(2)}, u32[]{:S(2)}) collective-permute-start(bf16[32,1,256]{2,1,0:T(2,128)(2,1)S(1)} %get-tuple-element.475), channel_id=1, source_target_pairs={{0,1},{1,2},{2,3},{3,4},{4,5},{5,6},{6,7},{7,0},{8,9},{9,10},{10,1... | collective-permute-start | bytes 49160 | tf_op jit(solution)/shard_map/while/body/eval_jaxpr/ppermute | solution.py:16
  70.3 12.2 %collective-permute-start.5 = (bf16[32,1,256]{2,0,1:T(8,128)(2,1)S(1)}, bf16[32,1,256]{2,0,1:T(8,128)(2,1)S(1)}, u32[]{:S(2)}, u32[]{:S(2)}) collective-permute-start(bf16[32,1,256]{2,0,1:T(8,128)(2,1)S(1)} %get-tuple-element.479), channel_id=1, source_target_pairs={{0,1},{1,2},{2,3},{3,4},{4,5},{5,6},{6,7},{7,0},{8,9},{9,10},{10,1... | collective-permute-start | bytes 49160 | tf_op jit(solution)/shard_map/while/body/eval_jaxpr/ppermute | solution.py:16
  70.7 10.4 %collective-permute-start.7 = (bf16[32,1,256]{2,0,1:T(8,128)(2,1)S(1)}, bf16[32,1,256]{2,0,1:T(8,128)(2,1)S(1)}, u32[]{:S(2)}, u32[]{:S(2)}) collective-permute-start(bf16[32,1,256]{2,0,1:T(8,128)(2,1)S(1)} %get-tuple-element.493), channel_id=1, source_target_pairs={{1,0},{2,1},{3,2},{4,3},{5,4},{6,5},{7,6},{0,7},{9,8},{10,9},{11,1... | collective-permute-start | bytes 49160 | tf_op jit(solution)/shard_map/while/body/eval_jaxpr/ppermute | solution.py:18
  74.2 6.9 %collective-permute-start.8 = (bf16[32,1,256]{2,0,1:T(8,128)(2,1)S(1)}, bf16[32,1,256]{2,0,1:T(8,128)(2,1)S(1)}, u32[]{:S(2)}, u32[]{:S(2)}) collective-permute-start(bf16[32,1,256]{2,0,1:T(8,128)(2,1)S(1)} %get-tuple-element.494), channel_id=1, source_target_pairs={{0,1},{1,2},{2,3},{3,4},{4,5},{5,6},{6,7},{7,0},{8,9},{9,10},{10,1... | collective-permute-start | bytes 49160 | tf_op jit(solution)/shard_map/while/body/eval_jaxpr/ppermute | solution.py:16
  77.5 5.1 %collective-permute-start.4 = (bf16[32,1,256]{2,0,1:T(8,128)(2,1)S(1)}, bf16[32,1,256]{2,0,1:T(8,128)(2,1)S(1)}, u32[]{:S(2)}, u32[]{:S(2)}) collective-permute-start(bf16[32,1,256]{2,0,1:T(8,128)(2,1)S(1)} %get-tuple-element.478), channel_id=1, source_target_pairs={{1,0},{2,1},{3,2},{4,3},{5,4},{6,5},{7,6},{0,7},{9,8},{10,9},{11,1... | collective-permute-start | bytes 49160 | tf_op jit(solution)/shard_map/while/body/eval_jaxpr/ppermute | solution.py:18
  84.9 7.2 %collective-permute-start.6 = (bf16[32,8,256]{2,1,0:T(8,128)(2,1)S(1)}, bf16[32,8,256]{2,1,0:T(8,128)(2,1)S(1)}, u32[]{:S(2)}, u32[]{:S(2)}) collective-permute-start(bf16[32,8,256]{2,1,0:T(8,128)(2,1)S(1)} %get-tuple-element.489), channel_id=1, source_target_pairs={{8,0},{16,8},{24,16},{9,1},{17,9},{25,17},{10,2},{18,10},{26,18},{... | collective-permute-start | bytes 393224 | tf_op jit(solution)/shard_map/while/body/eval_jaxpr/ppermute | solution.py:28
  93.1 13.0 %collective-permute-start = (bf16[32,1,256]{2,0,1:T(8,128)(2,1)S(1)}, bf16[32,1,256]{2,0,1:T(8,128)(2,1)S(1)}, u32[]{:S(2)}, u32[]{:S(2)}) collective-permute-start(bf16[32,1,256]{2,0,1:T(8,128)(2,1)S(1)} %get-tuple-element.464), channel_id=1, source_target_pairs={{1,0},{2,1},{3,2},{4,3},{5,4},{6,5},{7,6},{0,7},{9,8},{10,9},{11,1... | collective-permute-start | bytes 49160 | tf_op jit(solution)/shard_map/while/body/eval_jaxpr/ppermute | solution.py:18
  95.7 10.3 %collective-permute-start.1 = (bf16[32,1,256]{2,0,1:T(8,128)(2,1)S(1)}, bf16[32,1,256]{2,0,1:T(8,128)(2,1)S(1)}, u32[]{:S(2)}, u32[]{:S(2)}) collective-permute-start(bf16[32,1,256]{2,0,1:T(8,128)(2,1)S(1)} %get-tuple-element.465), channel_id=1, source_target_pairs={{0,1},{1,2},{2,3},{3,4},{4,5},{5,6},{6,7},{7,0},{8,9},{9,10},{10,1... | collective-permute-start | bytes 49160 | tf_op jit(solution)/shard_map/while/body/eval_jaxpr/ppermute | solution.py:16
  96.7 5.2 %collective-permute-start.2 = (bf16[32,1,256]{2,1,0:T(2,128)(2,1)S(1)}, bf16[32,1,256]{2,1,0:T(2,128)(2,1)S(1)}, u32[]{:S(2)}, u32[]{:S(2)}) collective-permute-start(bf16[32,1,256]{2,1,0:T(2,128)(2,1)S(1)} %get-tuple-element.474), channel_id=1, source_target_pairs={{1,0},{2,1},{3,2},{4,3},{5,4},{6,5},{7,6},{0,7},{9,8},{10,9},{11,1... | collective-permute-start | bytes 49160 | tf_op jit(solution)/shard_map/while/body/eval_jaxpr/ppermute | solution.py:18
  100.3 5.1 %collective-permute-start.3 = (bf16[32,1,256]{2,1,0:T(2,128)(2,1)S(1)}, bf16[32,1,256]{2,1,0:T(2,128)(2,1)S(1)}, u32[]{:S(2)}, u32[]{:S(2)}) collective-permute-start(bf16[32,1,256]{2,1,0:T(2,128)(2,1)S(1)} %get-tuple-element.475), channel_id=1, source_target_pairs={{0,1},{1,2},{2,3},{3,4},{4,5},{5,6},{6,7},{7,0},{8,9},{9,10},{10,1... | collective-permute-start | bytes 49160 | tf_op jit(solution)/shard_map/while/body/eval_jaxpr/ppermute | solution.py:16
  111.2 12.2 %collective-permute-start.5 = (bf16[32,1,256]{2,0,1:T(8,128)(2,1)S(1)}, bf16[32,1,256]{2,0,1:T(8,128)(2,1)S(1)}, u32[]{:S(2)}, u32[]{:S(2)}) collective-permute-start(bf16[32,1,256]{2,0,1:T(8,128)(2,1)S(1)} %get-tuple-element.479), channel_id=1, source_target_pairs={{0,1},{1,2},{2,3},{3,4},{4,5},{5,6},{6,7},{7,0},{8,9},{9,10},{10,1... | collective-permute-start | bytes 49160 | tf_op jit(solution)/shard_map/while/body/eval_jaxpr/ppermute | solution.py:16
  111.5 10.4 %collective-permute-start.7 = (bf16[32,1,256]{2,0,1:T(8,128)(2,1)S(1)}, bf16[32,1,256]{2,0,1:T(8,128)(2,1)S(1)}, u32[]{:S(2)}, u32[]{:S(2)}) collective-permute-start(bf16[32,1,256]{2,0,1:T(8,128)(2,1)S(1)} %get-tuple-element.493), channel_id=1, source_target_pairs={{1,0},{2,1},{3,2},{4,3},{5,4},{6,5},{7,6},{0,7},{9,8},{10,9},{11,1... | collective-permute-start | bytes 49160 | tf_op jit(solution)/shard_map/while/body/eval_jaxpr/ppermute | solution.py:18
  115.1 6.9 %collective-permute-start.8 = (bf16[32,1,256]{2,0,1:T(8,128)(2,1)S(1)}, bf16[32,1,256]{2,0,1:T(8,128)(2,1)S(1)}, u32[]{:S(2)}, u32[]{:S(2)}) collective-permute-start(bf16[32,1,256]{2,0,1:T(8,128)(2,1)S(1)} %get-tuple-element.494), channel_id=1, source_target_pairs={{0,1},{1,2},{2,3},{3,4},{4,5},{5,6},{6,7},{7,0},{8,9},{9,10},{10,1... | collective-permute-start | bytes 49160 | tf_op jit(solution)/shard_map/while/body/eval_jaxpr/ppermute | solution.py:16
  118.1 4.4 %copy-start.1 = (f32[3,3,256,256]{3,2,1,0:T(8,128)}, f32[3,3,256,256]{3,2,1,0:T(8,128)S(1)}, u32[]{:S(2)}) copy-start(f32[3,3,256,256]{3,2,1,0:T(8,128)S(1)} %fusion.369) | copy-start | bytes 7077892 | tf_op jit(solution)/shard_map/while
  118.3 5.1 %collective-permute-start.4 = (bf16[32,1,256]{2,0,1:T(8,128)(2,1)S(1)}, bf16[32,1,256]{2,0,1:T(8,128)(2,1)S(1)}, u32[]{:S(2)}, u32[]{:S(2)}) collective-permute-start(bf16[32,1,256]{2,0,1:T(8,128)(2,1)S(1)} %get-tuple-element.478), channel_id=1, source_target_pairs={{1,0},{2,1},{3,2},{4,3},{5,4},{6,5},{7,6},{0,7},{9,8},{10,9},{11,1... | collective-permute-start | bytes 49160 | tf_op jit(solution)/shard_map/while/body/eval_jaxpr/ppermute | solution.py:18
  125.7 7.5 %collective-permute-start.6 = (bf16[32,8,256]{2,1,0:T(8,128)(2,1)S(1)}, bf16[32,8,256]{2,1,0:T(8,128)(2,1)S(1)}, u32[]{:S(2)}, u32[]{:S(2)}) collective-permute-start(bf16[32,8,256]{2,1,0:T(8,128)(2,1)S(1)} %get-tuple-element.489), channel_id=1, source_target_pairs={{8,0},{16,8},{24,16},{9,1},{17,9},{25,17},{10,2},{18,10},{26,18},{... | collective-permute-start | bytes 393224 | tf_op jit(solution)/shard_map/while/body/eval_jaxpr/ppermute | solution.py:28
  134.2 13.0 %collective-permute-start = (bf16[32,1,256]{2,0,1:T(8,128)(2,1)S(1)}, bf16[32,1,256]{2,0,1:T(8,128)(2,1)S(1)}, u32[]{:S(2)}, u32[]{:S(2)}) collective-permute-start(bf16[32,1,256]{2,0,1:T(8,128)(2,1)S(1)} %get-tuple-element.464), channel_id=1, source_target_pairs={{1,0},{2,1},{3,2},{4,3},{5,4},{6,5},{7,6},{0,7},{9,8},{10,9},{11,1... | collective-permute-start | bytes 49160 | tf_op jit(solution)/shard_map/while/body/eval_jaxpr/ppermute | solution.py:18
  136.8 10.3 %collective-permute-start.1 = (bf16[32,1,256]{2,0,1:T(8,128)(2,1)S(1)}, bf16[32,1,256]{2,0,1:T(8,128)(2,1)S(1)}, u32[]{:S(2)}, u32[]{:S(2)}) collective-permute-start(bf16[32,1,256]{2,0,1:T(8,128)(2,1)S(1)} %get-tuple-element.465), channel_id=1, source_target_pairs={{0,1},{1,2},{2,3},{3,4},{4,5},{5,6},{6,7},{7,0},{8,9},{9,10},{10,1... | collective-permute-start | bytes 49160 | tf_op jit(solution)/shard_map/while/body/eval_jaxpr/ppermute | solution.py:16
  137.8 5.2 %collective-permute-start.2 = (bf16[32,1,256]{2,1,0:T(2,128)(2,1)S(1)}, bf16[32,1,256]{2,1,0:T(2,128)(2,1)S(1)}, u32[]{:S(2)}, u32[]{:S(2)}) collective-permute-start(bf16[32,1,256]{2,1,0:T(2,128)(2,1)S(1)} %get-tuple-element.474), channel_id=1, source_target_pairs={{1,0},{2,1},{3,2},{4,3},{5,4},{6,5},{7,6},{0,7},{9,8},{10,9},{11,1... | collective-permute-start | bytes 49160 | tf_op jit(solution)/shard_map/while/body/eval_jaxpr/ppermute | solution.py:18
  141.4 5.1 %collective-permute-start.3 = (bf16[32,1,256]{2,1,0:T(2,128)(2,1)S(1)}, bf16[32,1,256]{2,1,0:T(2,128)(2,1)S(1)}, u32[]{:S(2)}, u32[]{:S(2)}) collective-permute-start(bf16[32,1,256]{2,1,0:T(2,128)(2,1)S(1)} %get-tuple-element.475), channel_id=1, source_target_pairs={{0,1},{1,2},{2,3},{3,4},{4,5},{5,6},{6,7},{7,0},{8,9},{9,10},{10,1... | collective-permute-start | bytes 49160 | tf_op jit(solution)/shard_map/while/body/eval_jaxpr/ppermute | solution.py:16
  152.3 12.2 %collective-permute-start.5 = (bf16[32,1,256]{2,0,1:T(8,128)(2,1)S(1)}, bf16[32,1,256]{2,0,1:T(8,128)(2,1)S(1)}, u32[]{:S(2)}, u32[]{:S(2)}) collective-permute-start(bf16[32,1,256]{2,0,1:T(8,128)(2,1)S(1)} %get-tuple-element.479), channel_id=1, source_target_pairs={{0,1},{1,2},{2,3},{3,4},{4,5},{5,6},{6,7},{7,0},{8,9},{9,10},{10,1... | collective-permute-start | bytes 49160 | tf_op jit(solution)/shard_map/while/body/eval_jaxpr/ppermute | solution.py:16
  152.6 10.4 %collective-permute-start.7 = (bf16[32,1,256]{2,0,1:T(8,128)(2,1)S(1)}, bf16[32,1,256]{2,0,1:T(8,128)(2,1)S(1)}, u32[]{:S(2)}, u32[]{:S(2)}) collective-permute-start(bf16[32,1,256]{2,0,1:T(8,128)(2,1)S(1)} %get-tuple-element.493), channel_id=1, source_target_pairs={{1,0},{2,1},{3,2},{4,3},{5,4},{6,5},{7,6},{0,7},{9,8},{10,9},{11,1... | collective-permute-start | bytes 49160 | tf_op jit(solution)/shard_map/while/body/eval_jaxpr/ppermute | solution.py:18
  156.2 6.9 %collective-permute-start.8 = (bf16[32,1,256]{2,0,1:T(8,128)(2,1)S(1)}, bf16[32,1,256]{2,0,1:T(8,128)(2,1)S(1)}, u32[]{:S(2)}, u32[]{:S(2)}) collective-permute-start(bf16[32,1,256]{2,0,1:T(8,128)(2,1)S(1)} %get-tuple-element.494), channel_id=1, source_target_pairs={{0,1},{1,2},{2,3},{3,4},{4,5},{5,6},{6,7},{7,0},{8,9},{9,10},{10,1... | collective-permute-start | bytes 49160 | tf_op jit(solution)/shard_map/while/body/eval_jaxpr/ppermute | solution.py:16
  159.5 5.1 %collective-permute-start.4 = (bf16[32,1,256]{2,0,1:T(8,128)(2,1)S(1)}, bf16[32,1,256]{2,0,1:T(8,128)(2,1)S(1)}, u32[]{:S(2)}, u32[]{:S(2)}) collective-permute-start(bf16[32,1,256]{2,0,1:T(8,128)(2,1)S(1)} %get-tuple-element.478), channel_id=1, source_target_pairs={{1,0},{2,1},{3,2},{4,3},{5,4},{6,5},{7,6},{0,7},{9,8},{10,9},{11,1... | collective-permute-start | bytes 49160 | tf_op jit(solution)/shard_map/while/body/eval_jaxpr/ppermute | solution.py:18
  166.9 7.5 %collective-permute-start.6 = (bf16[32,8,256]{2,1,0:T(8,128)(2,1)S(1)}, bf16[32,8,256]{2,1,0:T(8,128)(2,1)S(1)}, u32[]{:S(2)}, u32[]{:S(2)}) collective-permute-start(bf16[32,8,256]{2,1,0:T(8,128)(2,1)S(1)} %get-tuple-element.489), channel_id=1, source_target_pairs={{8,0},{16,8},{24,16},{9,1},{17,9},{25,17},{10,2},{18,10},{26,18},{... | collective-permute-start | bytes 393224 | tf_op jit(solution)/shard_map/while/body/eval_jaxpr/ppermute | solution.py:28
  175.3 13.0 %collective-permute-start = (bf16[32,1,256]{2,0,1:T(8,128)(2,1)S(1)}, bf16[32,1,256]{2,0,1:T(8,128)(2,1)S(1)}, u32[]{:S(2)}, u32[]{:S(2)}) collective-permute-start(bf16[32,1,256]{2,0,1:T(8,128)(2,1)S(1)} %get-tuple-element.464), channel_id=1, source_target_pairs={{1,0},{2,1},{3,2},{4,3},{5,4},{6,5},{7,6},{0,7},{9,8},{10,9},{11,1... | collective-permute-start | bytes 49160 | tf_op jit(solution)/shard_map/while/body/eval_jaxpr/ppermute | solution.py:18
  178.0 10.3 %collective-permute-start.1 = (bf16[32,1,256]{2,0,1:T(8,128)(2,1)S(1)}, bf16[32,1,256]{2,0,1:T(8,128)(2,1)S(1)}, u32[]{:S(2)}, u32[]{:S(2)}) collective-permute-start(bf16[32,1,256]{2,0,1:T(8,128)(2,1)S(1)} %get-tuple-element.465), channel_id=1, source_target_pairs={{0,1},{1,2},{2,3},{3,4},{4,5},{5,6},{6,7},{7,0},{8,9},{9,10},{10,1... | collective-permute-start | bytes 49160 | tf_op jit(solution)/shard_map/while/body/eval_jaxpr/ppermute | solution.py:16
  178.9 5.2 %collective-permute-start.2 = (bf16[32,1,256]{2,1,0:T(2,128)(2,1)S(1)}, bf16[32,1,256]{2,1,0:T(2,128)(2,1)S(1)}, u32[]{:S(2)}, u32[]{:S(2)}) collective-permute-start(bf16[32,1,256]{2,1,0:T(2,128)(2,1)S(1)} %get-tuple-element.474), channel_id=1, source_target_pairs={{1,0},{2,1},{3,2},{4,3},{5,4},{6,5},{7,6},{0,7},{9,8},{10,9},{11,1... | collective-permute-start | bytes 49160 | tf_op jit(solution)/shard_map/while/body/eval_jaxpr/ppermute | solution.py:18
  182.5 5.1 %collective-permute-start.3 = (bf16[32,1,256]{2,1,0:T(2,128)(2,1)S(1)}, bf16[32,1,256]{2,1,0:T(2,128)(2,1)S(1)}, u32[]{:S(2)}, u32[]{:S(2)}) collective-permute-start(bf16[32,1,256]{2,1,0:T(2,128)(2,1)S(1)} %get-tuple-element.475), channel_id=1, source_target_pairs={{0,1},{1,2},{2,3},{3,4},{4,5},{5,6},{6,7},{7,0},{8,9},{9,10},{10,1... | collective-permute-start | bytes 49160 | tf_op jit(solution)/shard_map/while/body/eval_jaxpr/ppermute | solution.py:16
  193.4 12.2 %collective-permute-start.5 = (bf16[32,1,256]{2,0,1:T(8,128)(2,1)S(1)}, bf16[32,1,256]{2,0,1:T(8,128)(2,1)S(1)}, u32[]{:S(2)}, u32[]{:S(2)}) collective-permute-start(bf16[32,1,256]{2,0,1:T(8,128)(2,1)S(1)} %get-tuple-element.479), channel_id=1, source_target_pairs={{0,1},{1,2},{2,3},{3,4},{4,5},{5,6},{6,7},{7,0},{8,9},{9,10},{10,1... | collective-permute-start | bytes 49160 | tf_op jit(solution)/shard_map/while/body/eval_jaxpr/ppermute | solution.py:16
  193.8 10.4 %collective-permute-start.7 = (bf16[32,1,256]{2,0,1:T(8,128)(2,1)S(1)}, bf16[32,1,256]{2,0,1:T(8,128)(2,1)S(1)}, u32[]{:S(2)}, u32[]{:S(2)}) collective-permute-start(bf16[32,1,256]{2,0,1:T(8,128)(2,1)S(1)} %get-tuple-element.493), channel_id=1, source_target_pairs={{1,0},{2,1},{3,2},{4,3},{5,4},{6,5},{7,6},{0,7},{9,8},{10,9},{11,1... | collective-permute-start | bytes 49160 | tf_op jit(solution)/shard_map/while/body/eval_jaxpr/ppermute | solution.py:18
  197.3 6.9 %collective-permute-start.8 = (bf16[32,1,256]{2,0,1:T(8,128)(2,1)S(1)}, bf16[32,1,256]{2,0,1:T(8,128)(2,1)S(1)}, u32[]{:S(2)}, u32[]{:S(2)}) collective-permute-start(bf16[32,1,256]{2,0,1:T(8,128)(2,1)S(1)} %get-tuple-element.494), channel_id=1, source_target_pairs={{0,1},{1,2},{2,3},{3,4},{4,5},{5,6},{6,7},{7,0},{8,9},{9,10},{10,1... | collective-permute-start | bytes 49160 | tf_op jit(solution)/shard_map/while/body/eval_jaxpr/ppermute | solution.py:16
  200.6 5.1 %collective-permute-start.4 = (bf16[32,1,256]{2,0,1:T(8,128)(2,1)S(1)}, bf16[32,1,256]{2,0,1:T(8,128)(2,1)S(1)}, u32[]{:S(2)}, u32[]{:S(2)}) collective-permute-start(bf16[32,1,256]{2,0,1:T(8,128)(2,1)S(1)} %get-tuple-element.478), channel_id=1, source_target_pairs={{1,0},{2,1},{3,2},{4,3},{5,4},{6,5},{7,6},{0,7},{9,8},{10,9},{11,1... | collective-permute-start | bytes 49160 | tf_op jit(solution)/shard_map/while/body/eval_jaxpr/ppermute | solution.py:18
  208.0 7.5 %collective-permute-start.6 = (bf16[32,8,256]{2,1,0:T(8,128)(2,1)S(1)}, bf16[32,8,256]{2,1,0:T(8,128)(2,1)S(1)}, u32[]{:S(2)}, u32[]{:S(2)}) collective-permute-start(bf16[32,8,256]{2,1,0:T(8,128)(2,1)S(1)} %get-tuple-element.489), channel_id=1, source_target_pairs={{8,0},{16,8},{24,16},{9,1},{17,9},{25,17},{10,2},{18,10},{26,18},{... | collective-permute-start | bytes 393224 | tf_op jit(solution)/shard_map/while/body/eval_jaxpr/ppermute | solution.py:28
  (19 other events, 45.5 us)
Sparse Core Ops, SparseCore 0:
  215.6 109.0 all-reduce.6
where the time goes:
time: 337 us
  waiting for transfers between devices  148 us (44%)
  starting transfers between devices  75.5 us (22%)
  matrix products  49.7 us (15%)
  local copies, waits for them, and re-layouts  23.9 us (7%)
  other arithmetic  22.5 us (7%)
  between operations  14.1 us (4%)
    psum x1, waiting for transfers between devices, local(): summed_one, summed_two = lax.psum((grad_one, grad_two), 'lon')  109 us
    ppermute x20, starting transfers between devices, extended(): lax.ppermute(head, axis, [((i + 1) % count, i) for i in range(count)])  68.7 us
    dot_general x90, matrix products, convolve_back(): lax.dot_general(window, kernel[lat_off, lon_off], (((1,), (1,)), ((), ())...  20.2 us
    dot_general x90, matrix products, correlate(): lax.dot_general(window, flat_grad, (((0,), (0,)), ((), ())), preferred_el...  20.1 us
    ppermute x20, waiting for transfers between devices, extended(): lax.ppermute(tail, axis, [(i, (i + 1) % count) for i in range(count)])  17.7 us
    while x40, local copies, waits for them, and re-layouts  15.5 us
    ppermute x5, waiting for transfers between devices, from_behind(): return lax.ppermute(array, axis, pairs)  14.9 us
    dot_general x45, matrix products, convolve(): jnp.dot(window, kernel[lat_off, lon_off], preferred_element_type=jnp.floa...  9.34 us
  transfers between devices with their start and end apart: 46, of which 16 were waited for; matrix products, arithmetic and copies ran while one was open for 10% of the time, Pallas kernels for 0%

commit v1 on v0

v1 whole, which is shorter than its diff:
```python
import functools
import math

import jax
import jax.numpy as jnp
from jax import lax
from jax.experimental import pallas as pl
from jax.experimental.pallas import tpu as pltpu
from jax.sharding import PartitionSpec as P

MESH = pl.DeviceIdType.MESH
F32 = jnp.float32
BF16 = jnp.bfloat16
SPLIT = 2


def remote(src, dst, send_sem, recv_sem, where):
    return pltpu.make_async_remote_copy(
        src_ref=src,
        dst_ref=dst,
        send_sem=send_sem,
        recv_sem=recv_sem,
        device_id=where,
        device_id_type=MESH,
    )


def shift_lat(value, by, lat):
    rows, chans = value.shape
    rolled = pltpu.roll(value, by % rows, 0).reshape(rows // lat, lat, chans)
    row = lax.broadcasted_iota(jnp.int32, rolled.shape, 1)
    edge = 0 if by > 0 else lat - 1
    return jnp.where(row == edge, 0.0, rolled).reshape(rows, chans)


def three_by_three(read, weight, lat, contract):
    total = None
    for a in (1, 0, 2):
        part = None
        for b in range(3):
            term = lax.dot_general(
                read(b), weight(a, b), (((1,), (contract,)), ((), ())), preferred_element_type=F32
            )
            part = term if part is None else part + term
        if a != 1:
            part = shift_lat(part, 1 - a, lat)
        total = part if total is None else total + part
    return total


def kernel(
    dims, x_ref, w_ref, co_ref, act_ref, g_ref,
    xe, ce, slope, de, xt, ht, part, mine, pr, lr, rr, ls, rs,
    x_send, x_recv, co_send, c_send, c_recv, p_send, p_recv,
    l_send, l_recv, r_send, r_recv, f_send, f_recv,
):
    sections, lons, lat, factor = dims
    micro, cells, chans = x_ref.shape
    chunks, _, rows, _ = g_ref.shape
    line = lons // 2
    wide = cells + 2 * lat
    s = lax.axis_index("section")
    l = lax.axis_index("lon")
    k = l // 2
    core = l % 2
    left = lax.rem(l + lons - 1, lons)
    right = lax.rem(l + 1, lons)
    partner = (s, l + 1 - 2 * core)
    has_up = s < sections - 1
    has_down = s > 0

    barrier = pltpu.get_barrier_semaphore()

    def greet(sec, lon):
        pl.semaphore_signal(barrier, inc=1, device_id=(sec, lon), device_id_type=MESH)

    greet(s, left)
    greet(s, right)

    @pl.when(k > 0)
    def _():
        greet(s, l - 2)

    @pl.when(k < line - 1)
    def _():
        greet(s, l + 2)

    @pl.when(has_down)
    def _():
        for lon in (left, l, right):
            greet(s - 1, lon)

    @pl.when(has_up)
    def _():
        for lon in (left, l, right):
            greet(s + 1, lon)

    line_peers = jnp.where(k > 0, 1, 0) + jnp.where(k < line - 1, 1, 0)
    chain_peers = jnp.where(has_down, 3, 0) + jnp.where(has_up, 3, 0)
    pl.semaphore_wait(barrier, 2 + line_peers + chain_peers)

    def edge_right(src, dst, m, sec, send, recv):
        return remote(
            src.at[m, pl.ds(cells - 2 * lat, 2 * lat)], dst.at[m, pl.ds(0, 2 * lat)], send, recv, (sec, right)
        )

    def edge_left(src, dst, m, sec, send, recv):
        return remote(
            src.at[m, pl.ds(0, 2 * lat)],
            dst.at[m, pl.ds(cells + 2 * lat, 2 * lat)],
            send,
            recv,
            (sec, left),
        )

    def x_edges(m):
        return (
            edge_right(x_ref, xe, m, s, x_send.at[m, 0], x_recv.at[m, 0]),
            edge_left(x_ref, xe, m, s, x_send.at[m, 1], x_recv.at[m, 1]),
        )

    def co_edges(m):
        return (
            edge_right(co_ref, ce, m, s, co_send.at[m, 0], c_recv.at[m, 0]),
            edge_left(co_ref, ce, m, s, co_send.at[m, 1], c_recv.at[m, 1]),
        )

    def hops(m):
        return (
            edge_right(act_ref, ce, m, s - 1, c_send.at[m, 0], c_recv.at[m, 0]),
            edge_left(act_ref, ce, m, s - 1, c_send.at[m, 1], c_recv.at[m, 1]),
            remote(
                act_ref.at[m],
                ce.at[m, pl.ds(2 * lat, cells)],
                c_send.at[m, 2],
                c_recv.at[m, 2],
                (s - 1, l),
            ),
        )

    for m in range(micro):
        for copy in x_edges(m):
            copy.start()

    @pl.when(s == sections - 1)
    def _():
        for m in range(micro):
            for copy in co_edges(m):
                copy.start()
            ce[m, pl.ds(2 * lat, cells)] = co_ref[m]

    def lifted(value, dest, m):
        wide_value = value.astype(F32)
        for a in range(3):
            moved = wide_value if a == 1 else shift_lat(wide_value, 1 - a, lat)
            dest[m, a] = jnp.transpose(moved).astype(BF16)

    def forward(m, carry):
        xe[m, pl.ds(2 * lat, cells)] = x_ref[m]
        lifted(x_ref[m], xt, m)
        for copy in x_edges(m):
            copy.wait_recv()
        z = three_by_three(
            lambda b: xe[m, pl.ds(b * lat, wide)], lambda a, b: w_ref[3 * a + b], lat, 0
        )
        sig = jax.nn.sigmoid(z)
        slope[m] = sig * (1.0 + z * (1.0 - sig))
        hidden = (z * sig)[lat : lat + cells].astype(BF16)
        lifted(hidden, ht, m)
        return carry

    lax.fori_loop(0, micro, forward, 0)

    @pl.when(k == 0)
    def _():
        lr[...] = jnp.zeros_like(lr)

    @pl.when(k == line - 1)
    def _():
        rr[...] = jnp.zeros_like(rr)

    def chain(m, carry):
        @pl.when(has_up)
        def _():
            hops(m)[2].wait_recv()

        for copy in co_edges(m):
            copy.wait_recv()
        back = three_by_three(
            lambda b: ce[m, pl.ds(b * lat, wide)], lambda a, b: w_ref[17 - 3 * a - b], lat, 1
        )
        de[m] = (back * slope[m]).astype(BF16)
        down = three_by_three(
            lambda b: de[m, pl.ds(b * lat, cells)], lambda a, b: w_ref[8 - 3 * a - b], lat, 1
        )
        act_ref[m] = (ce[m, pl.ds(2 * lat, cells)].astype(F32) + down).astype(BF16)

        @pl.when(has_down)
        def _():
            for copy in hops(m):
                copy.start()

        return carry

    lax.fori_loop(0, micro, chain, 0)

    def pair(n):
        return remote(
            part.at[n, 1 - core], pr.at[n], p_send.at[n], p_recv.at[n], partner
        )

    def correlate(lifted_ref, grad_ref, base, margin):
        def one(b, carry):
            start = pl.multiple_of((margin + 1 - b) * lat, lat)
            for a in range(3):
                total = None
                for m in range(micro):
                    term = jnp.dot(
                        lifted_ref[m, a], grad_ref[m, pl.ds(start, cells)], preferred_element_type=F32
                    )
                    total = term if total is None else total + term
                tile = (total * factor).astype(BF16)
                lo = a * chans
                while lo < (a + 1) * chans:
                    block, inner = lo // rows, lo % rows
                    hi = min((block + 1) * rows, (a + 1) * chans)
                    part[base + SPLIT * b + block // 2, block % 2, inner : inner + hi - lo] = tile[
                        lo - a * chans : hi - a * chans
                    ]
                    lo = hi
            for q in range(SPLIT):
                pair(base + SPLIT * b + q).start()
            return carry

        lax.fori_loop(0, 3, one, 0)

    correlate(ht, ce, 0, 2)
    correlate(xt, de, 3 * SPLIT, 1)

    def to_right(n):
        return remote(ls.at[n], lr.at[n], l_send.at[n], l_recv.at[n], (s, l + 2))

    def to_left(n):
        return remote(rs.at[n], rr.at[n], r_send.at[n], r_recv.at[n], (s, l - 2))

    def final(n):
        return remote(g_ref.at[n, core], g_ref.at[n, core], f_send.at[n], f_recv.at[n], partner)

    def step(t, carry):
        @pl.when(t < chunks)
        def _():
            pair(t).wait_recv()
            mine[t] = part[t, core].astype(F32) + pr[t].astype(F32)

        i = t - k

        @pl.when((i >= 0) & (i < chunks))
        def _():
            @pl.when(k > 0)
            def _():
                to_right(i).wait_recv()

            @pl.when(k < line - 1)
            def _():
                ls[i] = (mine[i] + lr[i].astype(F32)).astype(BF16)
                to_right(i).start()

        j = t - (line - 1 - k)

        @pl.when((j >= 0) & (j < chunks))
        def _():
            @pl.when(k < line - 1)
            def _():
                to_left(j).wait_recv()

            @pl.when(k > 0)
            def _():
                rs[j] = (mine[j] + rr[j].astype(F32)).astype(BF16)
                to_left(j).start()

        n = t - (line - 1)

        @pl.when(n >= 0)
        def _():
            g_ref[n, core] = (mine[n] + lr[n].astype(F32) + rr[n].astype(F32)).astype(BF16)
            final(n).start()

        return carry

    lax.fori_loop(0, chunks + line - 1, step, 0)

    def settle(n, carry):
        pair(n).wait_send()
        final(n).wait_send()
        remote(
            g_ref.at[n, 1 - core], g_ref.at[n, 1 - core], f_send.at[n], f_recv.at[n], partner
        ).wait_recv()

        @pl.when(k < line - 1)
        def _():
            to_right(n).wait_send()

        @pl.when(k > 0)
        def _():
            to_left(n).wait_send()

        return carry

    lax.fori_loop(0, chunks, settle, 0)

    for m in range(micro):
        for copy in x_edges(m):
            copy.wait_send()

        @pl.when(s == sections - 1)
        def _():
            for copy in co_edges(m):
                copy.wait_send()

        @pl.when(has_down)
        def _():
            for copy in hops(m):
                copy.wait_send()


def local(sections, lons, section_inputs, weights, out_cot):
    _, micro, lat, cols, chans = section_inputs.shape
    factor = 1.0 / math.sqrt(micro * lat * cols * lons)
    cells = lat * cols
    x = section_inputs[0].transpose(0, 2, 1, 3).reshape(micro, cells, chans)
    co = out_cot.transpose(0, 2, 1, 3).reshape(micro, cells, chans)
    w = weights.reshape(18, chans, chans)
    chunks = 6 * SPLIT
    rows = 3 * chans // (2 * SPLIT)
    wide = cells + 2 * lat
    dma = pltpu.SemaphoreType.DMA
    vmem = pl.BlockSpec(memory_space=pltpu.VMEM)
    piece = (chunks, rows, chans)
    act, grads = pl.pallas_call(
        functools.partial(kernel, (sections, lons, lat, factor)),
        out_shape=(
            jax.ShapeDtypeStruct((micro, cells, chans), BF16),
            jax.ShapeDtypeStruct((chunks, 2, rows, chans), BF16),
        ),
        in_specs=[vmem] * 3,
        out_specs=(vmem, vmem),
        scratch_shapes=[
            pltpu.VMEM((micro, cells + 4 * lat, chans), BF16),
            pltpu.VMEM((micro, cells + 4 * lat, chans), BF16),
            pltpu.VMEM((micro, wide, chans), F32),
            pltpu.VMEM((micro, wide, chans), BF16),
            pltpu.VMEM((micro, 3, chans, cells), BF16),
            pltpu.VMEM((micro, 3, chans, cells), BF16),
            pltpu.VMEM((chunks, 2, rows, chans), BF16),
            pltpu.VMEM(piece, F32),
            pltpu.VMEM(piece, BF16),
            pltpu.VMEM(piece, BF16),
            pltpu.VMEM(piece, BF16),
            pltpu.VMEM(piece, BF16),
            pltpu.VMEM(piece, BF16),
            dma((micro, 2)),
            dma((micro, 2)),
            dma((micro, 2)),
            dma((micro, 3)),
            dma((micro, 3)),
        ]
        + [dma((chunks,))] * 8,
        compiler_params=pltpu.CompilerParams(
            collective_id=0, has_side_effects=True, vmem_limit_bytes=40 * 1024 * 1024
        ),
    )(x, w, co)
    act = act.reshape(micro, cols, lat, chans).transpose(0, 2, 1, 3)
    grads = grads.reshape(2, 3, 3, chans, chans)[::-1].transpose(0, 2, 1, 3, 4).astype(F32)
    return act[None], grads[None]


def solution(mesh):
    placed = (
        P("section", None, None, "lon", None),
        P("section", None, None, None, None, None),
        P(None, None, "lon", None),
    )
    return jax.shard_map(
        functools.partial(local, mesh.shape["section"], mesh.shape["lon"]),
        mesh=mesh,
        in_specs=placed,
        out_specs=(
            P("section", None, None, "lon", None),
            P("section", None, None, None, None, None),
        ),
        check_vma=False,
    )
```

time: 337 us -> 99.3 us (0.29)
  waiting for transfers between devices: 148 us -> 0 us
  Pallas kernels: 0 us -> 91 us
  starting transfers between devices: 75.5 us -> 0 us
  matrix products: 49.7 us -> 0 us
  other arithmetic: 22.5 us -> 2.71 us
  local copies, waits for them, and re-layouts: 23.9 us -> 4.67 us
  between operations: 14.1 us -> 0.67 us
    psum x1 -> x0, waiting for transfers between devices: 109 us -> none  [local(): summed_one, summed_two = lax.psum((grad_one, grad_two), 'lon')]
    pallas_call x0 -> x1, Pallas kernels: none -> 91 us  [local(): pl.pallas_call(functools.partial(kernel, (sections, lons, lat, factor)),...]
    ppermute x45 -> x0, starting transfers between devices: 75.5 us -> none  [the longest x20 68.7 us: extended(): lax.ppermute(head, axis, [((i + 1) % count, i) for i in range(count)])]
    dot_general x225 -> x0, matrix products: 49.7 us -> none  [the longest x90 20.2 us: convolve_back(): lax.dot_general(window, kernel[lat_off, lon_off], (((1,), (1,)), ((), ())...]
    ppermute x45 -> x0, waiting for transfers between devices: 39.5 us -> none  [the longest x20 17.7 us: extended(): lax.ppermute(tail, axis, [(i, (i + 1) % count) for i in range(count)])]
    while x40 -> x0, local copies, waits for them, and re-layouts: 15.5 us -> none
    add x10 -> x0, other arithmetic: 8.22 us -> none  [the longest x5 4.11 us: one_turn(): grad_one = grad_one + weight_mask * correlate(padded_in, preact_grad)]
    mul x1 -> x0, other arithmetic: 5 us -> none  [local(): weight_grads = (jnp.stack([summed_one, summed_two]) * factor)[None]]
  transfers between devices with their start and end apart: 46 -> 0, of which waited for: 16 -> 0; matrix products, arithmetic and copies ran while one was open for 10% -> 0% of each run, Pallas kernels for 0% -> 0%
where the time goes in v1:
time: 99.3 us; the launch traced here: 99 us
  Pallas kernels  91 us (92%)
  local copies, waits for them, and re-layouts  4.67 us (5%)
  other arithmetic  2.71 us (3%)
    pallas_call x1, Pallas kernels, local(): pl.pallas_call(functools.partial(kernel, (sections, lons, lat, factor)),...  91 us
    broadcast_in_dim x1, other arithmetic, local(): return (act[None], grads[None])  2.71 us

profile of v1, /device:TPU:0, one launch (start us, length us, event | category | flops | bytes accessed | tf_op | source)
XLA Modules:
  0.0 99.0 jit_solution(14864442433830487572)
XLA Ops:
  0.6 1.0 %copy.5 = bf16[2,8,32,256]{3,2,1,0:T(8,128)(2,1)S(1)} copy(bf16[2,8,32,256]{3,1,2,0:T(8,128)(2,1)} %bitcast.23) | data formatting | bytes 524288 | tf_op jit(solution)/shard_map/transpose | solution.py:330
  1.6 1.0 %copy.6 = bf16[2,8,32,256]{3,2,1,0:T(8,128)(2,1)S(1)} copy(bf16[2,8,32,256]{3,1,2,0:T(8,128)(2,1)} %bitcast.24) | data formatting | bytes 524288 | tf_op jit(solution)/shard_map/transpose | solution.py:331
  2.6 0.0 copy-start
  2.7 1.7 %copy-done = bf16[1,2,3,3,256,256]{5,4,3,2,1,0:T(8,128)(2,1)S(1)} copy-done((bf16[1,2,3,3,256,256]{5,4,3,2,1,0:T(8,128)(2,1)S(1)}, bf16[1,2,3,3,256,256]{5,4,3,2,1,0:T(8,128)(2,1)}, u32[]{:S(2)}) %copy-start) | copy-done | bytes 2359320
  4.3 91.0 %shard_map.50 = (bf16[2,256,256]{2,1,0:T(8,128)(2,1)S(1)}, bf16[12,2,192,256]{3,2,1,0:T(8,128)(2,1)S(1)}) custom-call(bf16[2,256,256]{2,1,0:T(8,128)(2,1)S(1)} %bitcast.20, bf16[18,256,256]{2,1,0:T(8,128)(2,1)S(1)} %bitcast.18, bf16[2,256,256]{2,1,0:T(8,128)(2,1)S(1)} %bitcast.21), custom_call_target="tpu_custom_call" | custom-call | tf_op jit(solution)/shard_map/pallas_call | solution.py:339
  95.3 0.9 copy.10
  96.2 0.2 copy.8
  96.3 2.7 %convert_bitcast_fusion = f32[1,2,3,3,256,256]{5,4,3,2,1,0:T(8,128)} fusion(bf16[2,3,3,256,256]{4,3,1,2,0:T(8,128)(2,1)S(1)} %copy.8), kind=kLoop, calls=%fused_computation | loop fusion | flops 1179648 | bytes 7077888 | tf_op jit(solution)/shard_map/broadcast_in_dim | solution.py:374
Async XLA Ops:
  2.6 1.7 %copy-start = (bf16[1,2,3,3,256,256]{5,4,3,2,1,0:T(8,128)(2,1)S(1)}, bf16[1,2,3,3,256,256]{5,4,3,2,1,0:T(8,128)(2,1)}, u32[]{:S(2)}) copy-start(bf16[1,2,3,3,256,256]{5,4,3,2,1,0:T(8,128)(2,1)} %param.4) | copy-start | bytes 7077892

commit v2 on v1

--- a/solution.py
+++ b/solution.py
@@ -11,7 +11,9 @@
 MESH = pl.DeviceIdType.MESH
 F32 = jnp.float32
 BF16 = jnp.bfloat16
-SPLIT = 2
+SPLIT = 4
+SLACK = 3
+SHIFT = 4
 
 
 def remote(src, dst, send_sem, recv_sem, where):
@@ -50,11 +52,11 @@
 
 def kernel(
     dims, x_ref, w_ref, co_ref, act_ref, g_ref,
-    xe, ce, slope, de, xt, ht, part, mine, pr, lr, rr, ls, rs,
+    xe, ce, slope, de, xt, ht, part, mine, pr, lr, rr, ls, rs, gift, got,
     x_send, x_recv, co_send, c_send, c_recv, p_send, p_recv,
-    l_send, l_recv, r_send, r_recv, f_send, f_recv,
+    l_send, l_recv, r_send, r_recv, f_send, f_recv, g_send, g_recv, o_send, o_recv,
 ):
-    sections, lons, lat, factor = dims
+    sections, lons, lat, factor, shares = dims
     micro, cells, chans = x_ref.shape
     chunks, _, rows, _ = g_ref.shape
     line = lons // 2
@@ -68,6 +70,12 @@
     partner = (s, l + 1 - 2 * core)
     has_up = s < sections - 1
     has_down = s > 0
+    mirror = (sections - 1 - s, l)
+    helps = s > sections - 1 - s
+    helped = s < sections - 1 - s
+    share = 0
+    for i, amount in enumerate(shares):
+        share = share + jnp.where(s == i, amount, 0)
 
     barrier = pltpu.get_barrier_semaphore()
 
@@ -95,9 +103,14 @@
         for lon in (left, l, right):
             greet(s + 1, lon)
 
+    @pl.when(helps | helped)
+    def _():
+        greet(*mirror)
+
+    mirror_peers = jnp.where(helps, 1, 0) + jnp.where(helped, 1, 0)
     line_peers = jnp.where(k > 0, 1, 0) + jnp.where(k < line - 1, 1, 0)
     chain_peers = jnp.where(has_down, 3, 0) + jnp.where(has_up, 3, 0)
-    pl.semaphore_wait(barrier, 2 + line_peers + chain_peers)
+    pl.semaphore_wait(barrier, 2 + line_peers + chain_peers + mirror_peers)
 
     def edge_right(src, dst, m, sec, send, recv):
         return remote(
@@ -155,7 +168,7 @@
             moved = wide_value if a == 1 else shift_lat(wide_value, 1 - a, lat)
             dest[m, a] = jnp.transpose(moved).astype(BF16)
 
-    def forward(m, carry):
+    def section(m, carry):
         xe[m, pl.ds(2 * lat, cells)] = x_ref[m]
         lifted(x_ref[m], xt, m)
         for copy in x_edges(m):
@@ -167,19 +180,7 @@
         slope[m] = sig * (1.0 + z * (1.0 - sig))
         hidden = (z * sig)[lat : lat + cells].astype(BF16)
         lifted(hidden, ht, m)
-        return carry
-
-    lax.fori_loop(0, micro, forward, 0)
-
-    @pl.when(k == 0)
-    def _():
-        lr[...] = jnp.zeros_like(lr)
-
-    @pl.when(k == line - 1)
-    def _():
-        rr[...] = jnp.zeros_like(rr)
-
-    def chain(m, carry):
+
         @pl.when(has_up)
         def _():
             hops(m)[2].wait_recv()
@@ -202,7 +203,15 @@
 
         return carry
 
-    lax.fori_loop(0, micro, chain, 0)
+    lax.fori_loop(0, micro, section, 0)
+
+    @pl.when(k == 0)
+    def _():
+        lr[...] = jnp.zeros_like(lr)
+
+    @pl.when(k == line - 1)
+    def _():
+        rr[...] = jnp.zeros_like(rr)
 
     def pair(n):
         return remote(
@@ -246,15 +255,36 @@
     def final(n):
         return remote(g_ref.at[n, core], g_ref.at[n, core], f_send.at[n], f_recv.at[n], partner)
 
+    def to_helper(i):
+        return remote(gift.at[i], got.at[i], g_send.at[i], g_recv.at[i], mirror)
+
+    def to_owner(i):
+        dest = g_ref.at[chunks - share + i, core]
+        return remote(gift.at[i], dest, o_send.at[i], o_recv.at[i], mirror)
+
+    length = chunks + jnp.where(helps, share, 0) - jnp.where(helped, share, 0)
+
     def step(t, carry):
-        @pl.when(t < chunks)
+        @pl.when((t < length) & (t < chunks))
         def _():
             pair(t).wait_recv()
             mine[t] = part[t, core].astype(F32) + pr[t].astype(F32)
 
-        i = t - k
-
-        @pl.when((i >= 0) & (i < chunks))
+        @pl.when(helped & (t < share))
+        def _():
+            at = chunks - share + t
+            pair(at).wait_recv()
+            gift[t] = (part[at, core].astype(F32) + pr[at].astype(F32)).astype(BF16)
+            to_helper(t).start()
+
+        @pl.when(helps & (t >= chunks) & (t < length))
+        def _():
+            to_helper(t - chunks).wait_recv()
+            mine[t] = got[t - chunks].astype(F32)
+
+        i = t - SLACK * k
+
+        @pl.when((i >= 0) & (i < length))
         def _():
             @pl.when(k > 0)
             def _():
@@ -265,9 +295,9 @@
                 ls[i] = (mine[i] + lr[i].astype(F32)).astype(BF16)
                 to_right(i).start()
 
-        j = t - (line - 1 - k)
-
-        @pl.when((j >= 0) & (j < chunks))
+        j = t - SLACK * (line - 1 - k)
+
+        @pl.when((j >= 0) & (j < length))
         def _():
             @pl.when(k < line - 1)
             def _():
@@ -278,16 +308,36 @@
                 rs[j] = (mine[j] + rr[j].astype(F32)).astype(BF16)
                 to_left(j).start()
 
-        n = t - (line - 1)
-
-        @pl.when(n >= 0)
+        n = t - SLACK * (line - 1)
+
+        @pl.when((n >= 0) & (n < chunks))
         def _():
             g_ref[n, core] = (mine[n] + lr[n].astype(F32) + rr[n].astype(F32)).astype(BF16)
             final(n).start()
 
+        @pl.when(n >= chunks)
+        def _():
+            gift[n - chunks] = (mine[n] + lr[n].astype(F32) + rr[n].astype(F32)).astype(BF16)
+            to_owner(n - chunks).start()
+
         return carry
 
-    lax.fori_loop(0, chunks + line - 1, step, 0)
+    lax.fori_loop(0, length + SLACK * (line - 1), step, 0)
+
+    def finish(i, carry):
+        @pl.when(helped)
+        def _():
+            to_owner(i).wait_recv()
+            final(chunks - share + i).start()
+            to_helper(i).wait_send()
+
+        @pl.when(helps)
+        def _():
+            to_owner(i).wait_send()
+
+        return carry
+
+    lax.fori_loop(0, share, finish, 0)
 
     def settle(n, carry):
         pair(n).wait_send()
@@ -296,6 +346,11 @@
             g_ref.at[n, 1 - core], g_ref.at[n, 1 - core], f_send.at[n], f_recv.at[n], partner
         ).wait_recv()
 
+        return carry
+
+    lax.fori_loop(0, chunks, settle, 0)
+
+    def settle_line(n, carry):
         @pl.when(k < line - 1)
         def _():
             to_right(n).wait_send()
@@ -306,7 +361,7 @@
 
         return carry
 
-    lax.fori_loop(0, chunks, settle, 0)
+    lax.fori_loop(0, length, settle_line, 0)
 
     for m in range(micro):
         for copy in x_edges(m):
@@ -336,8 +391,12 @@
     dma = pltpu.SemaphoreType.DMA
     vmem = pl.BlockSpec(memory_space=pltpu.VMEM)
     piece = (chunks, rows, chans)
+    gaps = [abs(sections - 1 - 2 * i) for i in range(sections)]
+    shares = [min(chunks // 2, SHIFT * gap) for gap in gaps]
+    extra = max(max(shares), 1)
+    longer = (chunks + extra, rows, chans)
     act, grads = pl.pallas_call(
-        functools.partial(kernel, (sections, lons, lat, factor)),
+        functools.partial(kernel, (sections, lons, lat, factor, shares)),
         out_shape=(
             jax.ShapeDtypeStruct((micro, cells, chans), BF16),
             jax.ShapeDtypeStruct((chunks, 2, rows, chans), BF16),
@@ -352,19 +411,24 @@
             pltpu.VMEM((micro, 3, chans, cells), BF16),
             pltpu.VMEM((micro, 3, chans, cells), BF16),
             pltpu.VMEM((chunks, 2, rows, chans), BF16),
-            pltpu.VMEM(piece, F32),
+            pltpu.VMEM(longer, F32),
             pltpu.VMEM(piece, BF16),
-            pltpu.VMEM(piece, BF16),
-            pltpu.VMEM(piece, BF16),
-            pltpu.VMEM(piece, BF16),
-            pltpu.VMEM(piece, BF16),
+            pltpu.VMEM(longer, BF16),
+            pltpu.VMEM(longer, BF16),
+            pltpu.VMEM(longer, BF16),
+            pltpu.VMEM(longer, BF16),
+            pltpu.VMEM((extra, rows, chans), BF16),
+            pltpu.VMEM((extra, rows, chans), BF16),
             dma((micro, 2)),
             dma((micro, 2)),
             dma((micro, 2)),
             dma((micro, 3)),
             dma((micro, 3)),
         ]
-        + [dma((chunks,))] * 8,
+        + [dma((chunks,))] * 2
+        + [dma((chunks + extra,))] * 4
+        + [dma((chunks,))] * 2
+        + [dma((extra,))] * 4,
         compiler_params=pltpu.CompilerParams(
             collective_id=0, has_side_effects=True, vmem_limit_bytes=40 * 1024 * 1024
         ),

time: 99.3 us -> 80.2 us (0.81)
  Pallas kernels: 91 us -> 71.9 us
    pallas_call x1, Pallas kernels: 91 us -> 71.9 us  [local(): pl.pallas_call(functools.partial(kernel, (sections, lons, lat, factor, sh...]
where the time goes in v2:
time: 80.2 us; the launch traced here: 80 us
  Pallas kernels  71.9 us (90%)
  local copies, waits for them, and re-layouts  4.67 us (6%)
  other arithmetic  2.71 us (3%)
    pallas_call x1, Pallas kernels, local(): pl.pallas_call(functools.partial(kernel, (sections, lons, lat, factor, sh...  71.9 us
    broadcast_in_dim x1, other arithmetic, local(): return (act[None], grads[None])  2.71 us
    unnamed x2, local copies, waits for them, and re-layouts  1.66 us

profile of v2, /device:TPU:0, one launch (start us, length us, event | category | flops | bytes accessed | tf_op | source)
XLA Modules:
  0.0 80.0 jit_solution(15703199705764320402)
XLA Ops:
  0.6 1.0 %copy.5 = bf16[2,8,32,256]{3,2,1,0:T(8,128)(2,1)S(1)} copy(bf16[2,8,32,256]{3,1,2,0:T(8,128)(2,1)} %bitcast.23) | data formatting | bytes 524288 | tf_op jit(solution)/shard_map/transpose | solution.py:385
  1.6 1.0 %copy.6 = bf16[2,8,32,256]{3,2,1,0:T(8,128)(2,1)S(1)} copy(bf16[2,8,32,256]{3,1,2,0:T(8,128)(2,1)} %bitcast.24) | data formatting | bytes 524288 | tf_op jit(solution)/shard_map/transpose | solution.py:386
  2.6 0.0 copy-start
  2.7 1.7 %copy-done = bf16[1,2,3,3,256,256]{5,4,3,2,1,0:T(8,128)(2,1)S(1)} copy-done((bf16[1,2,3,3,256,256]{5,4,3,2,1,0:T(8,128)(2,1)S(1)}, bf16[1,2,3,3,256,256]{5,4,3,2,1,0:T(8,128)(2,1)}, u32[]{:S(2)}) %copy-start) | copy-done | bytes 2359320
  4.3 71.9 %shard_map.50 = (bf16[2,256,256]{2,1,0:T(8,128)(2,1)S(1)}, bf16[24,2,96,256]{3,2,1,0:T(8,128)(2,1)S(1)}) custom-call(bf16[2,256,256]{2,1,0:T(8,128)(2,1)S(1)} %bitcast.20, bf16[18,256,256]{2,1,0:T(8,128)(2,1)S(1)} %bitcast.18, bf16[2,256,256]{2,1,0:T(8,128)(2,1)S(1)} %bitcast.21), custom_call_target="tpu_custom_call" | custom-call | tf_op jit(solution)/shard_map/pallas_call | solution.py:398
  76.3 0.9 %copy.10 = bf16[2,8,32,256]{3,1,2,0:T(8,128)(2,1)} copy(bf16[2,8,32,256]{3,2,1,0:T(8,128)(2,1)S(1)} %bitcast.22) | data formatting | bytes 524288 | tf_op jit(solution)/shard_map/reshape | solution.py:436
  77.1 0.2 copy.8
  77.3 2.7 %convert_bitcast_fusion = f32[1,2,3,3,256,256]{5,4,3,2,1,0:T(8,128)} fusion(bf16[2,3,3,256,256]{4,3,1,2,0:T(8,128)(2,1)S(1)} %copy.8), kind=kLoop, calls=%fused_computation | loop fusion | flops 1179648 | bytes 7077888 | tf_op jit(solution)/shard_map/broadcast_in_dim | solution.py:438
Async XLA Ops:
  2.6 1.7 %copy-start = (bf16[1,2,3,3,256,256]{5,4,3,2,1,0:T(8,128)(2,1)S(1)}, bf16[1,2,3,3,256,256]{5,4,3,2,1,0:T(8,128)(2,1)}, u32[]{:S(2)}) copy-start(bf16[1,2,3,3,256,256]{5,4,3,2,1,0:T(8,128)(2,1)} %param.4) | copy-start | bytes 7077892

commit v3 on v2

--- a/solution.py
+++ b/solution.py
@@ -13,7 +13,7 @@
 BF16 = jnp.bfloat16
 SPLIT = 4
 SLACK = 3
-SHIFT = 4
+SHIFT = 3
 
 
 def remote(src, dst, send_sem, recv_sem, where):
@@ -52,7 +52,7 @@
 
 def kernel(
     dims, x_ref, w_ref, co_ref, act_ref, g_ref,
-    xe, ce, slope, de, xt, ht, part, mine, pr, lr, rr, ls, rs, gift, got,
+    xe, ce, slope, de, xt, ht, part, mine, pr, lr, rr, ls, rs, gift, got, held,
     x_send, x_recv, co_send, c_send, c_recv, p_send, p_recv,
     l_send, l_recv, r_send, r_recv, f_send, f_recv, g_send, g_recv, o_send, o_recv,
 ):
@@ -170,7 +170,6 @@
 
     def section(m, carry):
         xe[m, pl.ds(2 * lat, cells)] = x_ref[m]
-        lifted(x_ref[m], xt, m)
         for copy in x_edges(m):
             copy.wait_recv()
         z = three_by_three(
@@ -178,8 +177,13 @@
         )
         sig = jax.nn.sigmoid(z)
         slope[m] = sig * (1.0 + z * (1.0 - sig))
-        hidden = (z * sig)[lat : lat + cells].astype(BF16)
-        lifted(hidden, ht, m)
+        held[m] = (z * sig)[lat : lat + cells].astype(BF16)
+
+        def lift():
+            lifted(xe[m, pl.ds(2 * lat, cells)], xt, m)
+            lifted(held[m], ht, m)
+
+        pl.when(has_up)(lift)
 
         @pl.when(has_up)
         def _():
@@ -200,6 +204,8 @@
         def _():
             for copy in hops(m):
                 copy.start()
+
+        pl.when(s == sections - 1)(lift)
 
         return carry
 
@@ -419,6 +425,7 @@
             pltpu.VMEM(longer, BF16),
             pltpu.VMEM((extra, rows, chans), BF16),
             pltpu.VMEM((extra, rows, chans), BF16),
+            pltpu.VMEM((micro, cells, chans), BF16),
             dma((micro, 2)),
             dma((micro, 2)),
             dma((micro, 2)),

time: 80.2 us -> 76.7 us (0.956)
  Pallas kernels: 71.9 us -> 68.4 us
    pallas_call x1, Pallas kernels: 71.9 us -> 68.4 us  [local(): pl.pallas_call(functools.partial(kernel, (sections, lons, lat, factor, sh...]
where the time goes in v3:
time: 76.7 us; the launch traced here: 76.5 us
  Pallas kernels  68.4 us (89%)
  local copies, waits for them, and re-layouts  4.67 us (6%)
  other arithmetic  2.71 us (4%)
    pallas_call x1, Pallas kernels, local(): pl.pallas_call(functools.partial(kernel, (sections, lons, lat, factor, sh...  68.4 us
    broadcast_in_dim x1, other arithmetic, local(): return (act[None], grads[None])  2.71 us
    unnamed x2, local copies, waits for them, and re-layouts  1.66 us

profile of v3, /device:TPU:0, one launch (start us, length us, event | category | flops | bytes accessed | tf_op | source)
XLA Modules:
  0.0 76.5 jit_solution(6926299634613755558)
XLA Ops:
  0.6 1.0 %copy.5 = bf16[2,8,32,256]{3,2,1,0:T(8,128)(2,1)S(1)} copy(bf16[2,8,32,256]{3,1,2,0:T(8,128)(2,1)} %bitcast.23) | data formatting | bytes 524288 | tf_op jit(solution)/shard_map/transpose | solution.py:391
  1.6 1.0 %copy.6 = bf16[2,8,32,256]{3,2,1,0:T(8,128)(2,1)S(1)} copy(bf16[2,8,32,256]{3,1,2,0:T(8,128)(2,1)} %bitcast.24) | data formatting | bytes 524288 | tf_op jit(solution)/shard_map/transpose | solution.py:392
  2.6 0.0 copy-start
  2.7 1.7 %copy-done = bf16[1,2,3,3,256,256]{5,4,3,2,1,0:T(8,128)(2,1)S(1)} copy-done((bf16[1,2,3,3,256,256]{5,4,3,2,1,0:T(8,128)(2,1)S(1)}, bf16[1,2,3,3,256,256]{5,4,3,2,1,0:T(8,128)(2,1)}, u32[]{:S(2)}) %copy-start) | copy-done | bytes 2359320
  4.3 68.4 %shard_map.50 = (bf16[2,256,256]{2,1,0:T(8,128)(2,1)S(1)}, bf16[24,2,96,256]{3,2,1,0:T(8,128)(2,1)S(1)}) custom-call(bf16[2,256,256]{2,1,0:T(8,128)(2,1)S(1)} %bitcast.20, bf16[18,256,256]{2,1,0:T(8,128)(2,1)S(1)} %bitcast.18, bf16[2,256,256]{2,1,0:T(8,128)(2,1)S(1)} %bitcast.21), custom_call_target="tpu_custom_call" | custom-call | tf_op jit(solution)/shard_map/pallas_call | solution.py:404
  72.8 0.9 %copy.10 = bf16[2,8,32,256]{3,1,2,0:T(8,128)(2,1)} copy(bf16[2,8,32,256]{3,2,1,0:T(8,128)(2,1)S(1)} %bitcast.22) | data formatting | bytes 524288 | tf_op jit(solution)/shard_map/reshape | solution.py:443
  73.6 0.2 copy.8
  73.8 2.7 %convert_bitcast_fusion = f32[1,2,3,3,256,256]{5,4,3,2,1,0:T(8,128)} fusion(bf16[2,3,3,256,256]{4,3,1,2,0:T(8,128)(2,1)S(1)} %copy.8), kind=kLoop, calls=%fused_computation | loop fusion | flops 1179648 | bytes 7077888 | tf_op jit(solution)/shard_map/broadcast_in_dim | solution.py:445
Async XLA Ops:
  2.6 1.7 %copy-start = (bf16[1,2,3,3,256,256]{5,4,3,2,1,0:T(8,128)(2,1)S(1)}, bf16[1,2,3,3,256,256]{5,4,3,2,1,0:T(8,128)(2,1)}, u32[]{:S(2)}) copy-start(bf16[1,2,3,3,256,256]{5,4,3,2,1,0:T(8,128)(2,1)} %param.4) | copy-start | bytes 7077892
